TPU v7x, 32 devices: a whole 2x2x4 slice. The times are simulated.
32 devices in a mesh: groups: 2 (over x), rows: 16 (over z, y, core).
Axes of the slice: x: 2, y: 2, z: 4, core: 2. Of those that a mesh axis runs over, the one named last changes fastest.
Arguments:
- rhs: float32 [2, 65536], P(None, ('groups', 'rows')), parts along dimension 1
- geometry: float32 [6, 65536], P(None, ('groups', 'rows')), parts along dimension 1, as said below
- proxies: float32 [6, 32768], P(None, ('groups', 'rows')), parts along dimension 1, as said below
- basis_in: bfloat16 [512, 2, 64, 128], P(('groups', 'rows')), parts along dimension 0, may hold values from -0.5 to 0.5
- basis_out: bfloat16 [512, 2, 64, 128], P(('groups', 'rows')), parts along dimension 0, may hold values from -6 to 6
- far_tasks: int32 [2, 6144], P(None, ('groups', 'rows')), parts along dimension 1, may hold values from 0 to 255, as said below
- near_tiles: int32 [4, 512], P(None, ('groups', 'rows')), parts along dimension 1, may hold values from 0 to 255, as said below
Outputs:
- second_vector: float32 [2, 65536], P(None, ('groups', 'rows')), parts along dimension 1
- third_vector: float32 [2, 65536], P(None, ('groups', 'rows')), parts along dimension 1
- hessenberg: float32 [10], P('groups'), parts along dimension 0
There are 2 independent parts, one for each index of `groups`. A program takes and returns all parts, laid end to end along the dimension named above; each array names one. Nothing has to cross between parts.
Inputs may be any that keep to these rules, and one draw needn't show every extreme that they name: `far_tasks`: each row cluster is the row of exactly 36, 12 or 6 blocks, for an eighth, three eighths and half of the clusters; the source b of a block with row a satisfies b = a + o modulo 256 with 16 < o < 240; each device holds 192 blocks, of which at most 36 have their row clusters on any one device, and some device holds exactly 36 such blocks for some device. `near_tiles`: tile 0 of cluster r is r itself; the others are distinct clusters r + o modulo 256 with 1 <= |o| <= 16. `geometry`: panels of cluster c lie around a point of a sphere of radius 6 that moves slowly with c; areas are positive. `proxies`: proxies of cluster c lie around the same point as its panels; weights are positive.
All inputs are finite; a program needn't handle non-finite values.
Results may differ from a plain program's by a relative error of at most 0.0055.
The roundings to bfloat16 on the way count: a program that leaves them out, or rounds other values in their place, can miss the bound.
Values may be sent and summed in bfloat16 or wider, within the bound.
A program may use at most 128 MiB of HBM per device.

v0:
```python
import jax
import jax.numpy as jnp
from jax import lax
from jax.sharding import PartitionSpec as P

coulomb = 1.0 / (4.0 * 3.141592653589793)
kappa = 0.5
ratio = 4.0
eps = 1e-06


def with_halo(cells, sides, width):
    for axis, dim in sides:
        count = lax.axis_size(axis)
        head = lax.slice_in_dim(cells, 0, width, axis=dim)
        tail = lax.slice_in_dim(cells, cells.shape[dim] - width, cells.shape[dim], axis=dim)
        cells = jnp.concatenate(
            [
                lax.ppermute(tail, axis, [(i, (i + 1) % count) for i in range(count)]),
                cells,
                lax.ppermute(head, axis, [((i + 1) % count, i) for i in range(count)]),
            ],
            axis=dim,
        )
    return cells


def kernel_blocks(target, source):
    diff_x = target[0][:, None] - source[0][None, :]
    diff_y = target[1][:, None] - source[1][None, :]
    diff_z = target[2][:, None] - source[2][None, :]
    dist_sq = (
        diff_x * diff_x
        + diff_y * diff_y
        + diff_z * diff_z
        + target[5][:, None]
        + source[5][None, :]
    )
    radius = jnp.sqrt(dist_sq)
    inverse = 1.0 / radius
    cube = inverse * inverse * inverse
    screen = jnp.exp(-kappa * radius)
    growth = (1.0 + kappa * radius) * screen
    weight = source[5][None, :]
    src_nx = (jnp.sin(source[3]) * jnp.cos(source[4]))[None, :]
    src_ny = (jnp.sin(source[3]) * jnp.sin(source[4]))[None, :]
    src_nz = jnp.cos(source[3])[None, :]
    tgt_nx = (jnp.sin(target[3]) * jnp.cos(target[4]))[:, None]
    tgt_ny = (jnp.sin(target[3]) * jnp.sin(target[4]))[:, None]
    tgt_nz = jnp.cos(target[3])[:, None]
    single = coulomb * weight * inverse
    double = coulomb * weight * (diff_x * src_nx + diff_y * src_ny + diff_z * src_nz) * cube
    adjoint = -coulomb * weight * (diff_x * tgt_nx + diff_y * tgt_ny + diff_z * tgt_nz) * cube
    upper = jnp.stack([double - ratio * double * growth, single * screen - single], 1)
    lower = jnp.stack([adjoint - adjoint * growth, adjoint - adjoint * growth / ratio], 1)
    return jnp.stack([upper, lower], 0)


def shards(rhs, geometry, proxies, basis_in, basis_out, far_tasks, near_tiles):
    clusters = basis_in.shape[0]
    rank = basis_in.shape[2]
    panels = geometry.shape[1]
    members = panels // clusters
    devices = lax.axis_size("rows")
    total_clusters = clusters * devices
    first_cluster = lax.axis_index("rows") * clusters
    entries = 2.0 * panels * devices
    cluster_ids = jnp.arange(clusters, dtype=jnp.int32)
    wide_geometry = with_halo(geometry, (("rows", 1),), panels)
    wide_geo = wide_geometry.reshape(6, 3 * clusters, members)
    local_geo = geometry.reshape(6, clusters, members)
    near_local = (near_tiles - first_cluster + clusters) % total_clusters

    def tile_row(sources):
        return jax.vmap(lambda a, b: kernel_blocks(local_geo[:, a], wide_geo[:, b]))(
            cluster_ids, sources
        )

    near_mats = lax.map(tile_row, near_local)
    all_proxy = lax.all_gather(proxies, "rows", axis=1, tiled=True).reshape(6, total_clusters, rank)
    task_rows = far_tasks[0]
    task_srcs = far_tasks[1]
    task_count = task_rows.shape[0]
    per_step = task_count // clusters

    def block_group(pair):
        mats = jax.vmap(lambda a, b: kernel_blocks(all_proxy[:, a], all_proxy[:, b]))(
            pair[0], pair[1]
        )
        return mats.reshape(per_step, 2 * rank, 2 * rank).astype(jnp.bfloat16)

    coupled = lax.map(
        block_group, (task_rows.reshape(clusters, per_step), task_srcs.reshape(clusters, per_step))
    )
    coupled = coupled.reshape(task_count, 2 * rank, 2 * rank)

    def expansions(moments_all):
        picked = moments_all[task_srcs]
        terms = jnp.einsum("tab,tb->ta", coupled, picked, preferred_element_type=jnp.float32)
        wanted = jnp.arange(clusters * lax.axis_size("rows"), dtype=jnp.int32)
        selector = (task_rows[None, :] == wanted[:, None]).astype(jnp.float32)
        return lax.psum_scatter(
            jnp.dot(selector, terms, precision=lax.Precision.HIGHEST),
            "rows",
            scatter_dimension=0,
            tiled=True,
        )

    def operate(density):
        wide = with_halo(density, (("rows", 1),), panels)
        neighbours = wide.reshape(2, 3 * clusters, members)[:, near_local]
        near = jnp.einsum(
            "tckilj,ltcj->kci", near_mats, neighbours, precision=lax.Precision.HIGHEST
        )
        low = density.astype(jnp.bfloat16).reshape(2, clusters, members)
        moments = jnp.einsum("ckrp,kcp->ckr", basis_in, low, preferred_element_type=jnp.float32)
        moments = moments.astype(jnp.bfloat16).reshape(clusters, 2 * rank)
        moments_all = lax.all_gather(moments, "rows", axis=0, tiled=True)
        local_exp = expansions(moments_all).astype(jnp.bfloat16).reshape(clusters, 2, rank)
        far = jnp.einsum("ckrp,ckr->kcp", basis_out, local_exp, preferred_element_type=jnp.float32)
        diag = jnp.stack([(1.0 + ratio) / 2.0 * density[0], (1.0 + 1.0 / ratio) / 2.0 * density[1]])
        return diag + near.reshape(2, panels) + far.reshape(2, panels)

    def orthogonal(vectors, image):
        local_proj = jnp.stack([jnp.sum(vector * image) for vector in vectors])
        coeffs = lax.psum(local_proj, "rows") / entries
        for index in range(len(vectors)):
            image = image - coeffs[index] * vectors[index]
        length_sq = lax.psum(jnp.sum(image * image), "rows") / entries
        length = jnp.sqrt(length_sq + eps)
        return (coeffs, length, image / length)

    rhs_sq = lax.psum(jnp.sum(rhs * rhs), "rows")
    first = rhs / jnp.sqrt(rhs_sq / entries + eps)
    coeffs_one, h21, second_vector = orthogonal([first], operate(first))
    coeffs_two, h32, third_vector = orthogonal([first, second_vector], operate(second_vector))
    hessenberg = jnp.stack([coeffs_one[0], h21, coeffs_two[0], coeffs_two[1], h32])
    return (second_vector, third_vector, hessenberg)


def solution(mesh):
    return jax.shard_map(
        shards,
        mesh=mesh,
        in_specs=(
            P(None, ("groups", "rows")),
            P(None, ("groups", "rows")),
            P(None, ("groups", "rows")),
            P(("groups", "rows"), None, None, None),
            P(("groups", "rows"), None, None, None),
            P(None, ("groups", "rows")),
            P(None, ("groups", "rows")),
        ),
        out_specs=(P(None, ("groups", "rows")), P(None, ("groups", "rows")), P("groups")),
        check_vma=False,
    )
```

profile of v0, /device:TPU:0, one launch (start us, length us, event | category | flops | bytes accessed | tf_op | source)
XLA Modules:
  0.0 466.8 jit_solution(3478564062381883557)
XLA Ops:
  7.2 1.4 multiply_reduce_fusion.5
  8.6 35.5 %psum.35 = f32[]{:T(128)} all-reduce(f32[]{:T(128)} %multiply_reduce_fusion.5), channel_id=1, replica_groups=mesh['groups'=2,'rows'=16] {'rows'}, use_global_device_ids=true, to_apply=%region_1.2 | all-reduce | flops 1 | bytes 8 | tf_op jit(solution)/shard_map/psum | solution.py:133
  45.6 4.4 collective-permute-start.1
  50.1 4.4 collective-permute-start.3
  56.2 18.9 %all_gather.9 = f32[6,16384]{1,0:T(8,128)S(1)} all-gather(f32[6,1024]{1,0:T(8,128)} %param.13), channel_id=1, replica_groups=mesh['groups'=2,'rows'=16] {'rows'}, dimensions={1}, use_global_device_ids=true | all-gather | bytes 417792 | tf_op jit(solution)/shard_map/all_gather | solution.py:80
  75.9 88.2 %while.26 = (s32[]{:T(128)}, bf16[16,12,128,128]{3,2,1,0:T(8,128)(2,1)}, s32[16,12]{1,0:T(8,128)S(1)}, f32[6,256,64]{2,0,1:T(8,128)S(1)}, s32[16,12]{1,0:T(8,128)S(1)}, /*index=5*/s32[]{:T(128)}) while((s32[]{:T(128)}, bf16[16,12,128,128]{3,2,1,0:T(8,128)(2,1)}, s32[16,12]{1,0:T(8,128)S(1)}, f32[6,256,64]{2,0,1:T(8,128)S(1)}, ...), condition=%wide.region_5.6_spmd, body=%wide.region_4.5_spmd.sunk | while | flops 2609786 | bytes 4633641 | solution.py:92
  78.0 1.1 subtract_convert_fusion.4
  79.5 0.8 copy.174
  83.5 1.1 subtract_convert_fusion.4
  85.0 0.8 copy.174
  89.1 1.1 subtract_convert_fusion.4
  90.5 0.8 copy.174
  94.6 1.1 subtract_convert_fusion.4
  96.0 0.8 copy.174
  100.1 1.1 subtract_convert_fusion.4
  101.5 0.8 copy.174
  105.6 1.1 subtract_convert_fusion.4
  107.0 0.8 copy.174
  111.1 1.1 subtract_convert_fusion.4
  112.5 0.8 copy.174
  116.6 1.1 subtract_convert_fusion.4
  118.0 0.8 copy.174
  122.1 1.1 subtract_convert_fusion.4
  123.6 0.8 copy.174
  127.6 1.1 subtract_convert_fusion.4
  129.1 0.8 copy.174
  133.1 1.1 subtract_convert_fusion.4
  134.6 0.8 copy.174
  138.6 1.1 subtract_convert_fusion.4
  140.1 0.8 copy.174
  144.1 1.1 subtract_convert_fusion.4
  145.6 0.8 copy.174
  149.7 1.1 subtract_convert_fusion.4
  151.1 0.8 copy.174
  155.2 1.1 subtract_convert_fusion.4
  156.6 0.8 copy.174
  160.7 1.1 subtract_convert_fusion.4
  162.1 0.8 copy.174
  164.6 19.6 %all_gather.10 = bf16[256,128]{1,0:T(8,128)(2,1)S(1)} all-gather(bf16[16,128]{1,0:T(8,128)(2,1)S(1)} %reshape.549), channel_id=1, replica_groups=mesh['groups'=2,'rows'=16] {'rows'}, dimensions={0}, use_global_device_ids=true | all-gather | bytes 69632 | tf_op jit(solution)/shard_map/all_gather | solution.py:118
  185.0 6.1 %fusion.44 = f32[192,1,128]{2,1,0:T(1,128)S(1)} fusion(bf16[192,128,128]{2,1,0:T(8,128)(2,1)} %bitcast.275, bf16[192,128,1]{1,0,2:T(8,128)(2,1)S(1)} %bitcast.304), kind=kOutput, calls=%fused_computation.137 | convolution fusion | flops 6291456 | bytes 6438912 | tf_op jit(solution)/shard_map/tab,tb->ta/dot_general | solution.py:99
  191.1 1.0 fusion.39
  194.4 23.6 %while.25 = (s32[]{:T(128)}, f32[4,16,2,128,2,128]{5,3,0,4,2,1:T(8,128)}, s32[4,16]{1,0:T(4,128)S(1)}, f32[6,48,128]{2,0,1:T(8,128)S(1)}, f32[16,6,1,128]{3,0,1,...) while((s32[]{:T(128)}, ...), condition=%wide.region_3.4_spmd, body=%wide.region_2.3_spmd.sunk | while | flops 12853330 | bytes 21390240 | solution.py:79
  195.5 2.1 multiply_subtract_fusion.9
  198.1 2.2 copy_dynamic-update-slice_fusion.2
  201.4 2.1 multiply_subtract_fusion.9
  204.0 2.2 copy_dynamic-update-slice_fusion.2
  207.3 2.1 multiply_subtract_fusion.9
  209.9 2.2 copy_dynamic-update-slice_fusion.2
  213.2 2.1 multiply_subtract_fusion.9
  215.8 2.2 copy_dynamic-update-slice_fusion.2
  218.0 16.3 %fusion.48 = f32[16,1,2,128,1,1]{3,1,5,4,2,0:T(1,128)S(1)} fusion(f32[4,16,2,128,2,128]{5,3,0,4,2,1:T(8,128)} %get-tuple-element.176, f32[2,4,16,128,1,1]{3,0,2,1,4,5:T(2,128)S(1)} %bitcast.307), kind=kOutput, calls=%fused_computation.141 | convolution fusion | flops 50331648 | bytes 16859136 | tf_op jit(solution)/shard_map/tckilj,ltcj->kci/dot_general | solution.py:112
  234.2 10.4 %reduce-scatter.3.cloned.1.call-done = f32[16,128]{1,0:T(8,128)} async-done(((f32[256,128]{1,0:T(8,128)}), f32[16,128]{1,0:T(8,128)}) %reduce-scatter.3.cloned.1.call-update) | async-done | bytes 8208 | tf_op jit(solution)/shard_map/reduce_scatter | solution.py:102
  246.3 30.1 %psum.36 = f32[1]{0:T(128)} all-reduce(f32[1]{0:T(128)} %bitcast.51), channel_id=1, replica_groups=mesh['groups'=2,'rows'=16] {'rows'}, use_global_device_ids=true, to_apply=%region_8.9 | all-reduce | flops 1 | bytes 8 | tf_op jit(solution)/shard_map/psum | solution.py:126
  277.7 30.1 %psum.37 = f32[]{:T(128)} all-reduce(f32[]{:T(128)} %multiply_reduce_fusion.3), channel_id=1, replica_groups=mesh['groups'=2,'rows'=16] {'rows'}, use_global_device_ids=true, to_apply=%region_10.11 | all-reduce | flops 1 | bytes 8 | tf_op jit(solution)/shard_map/psum | solution.py:129
  308.6 4.4 collective-permute-start.5
  313.6 17.5 %all_gather.11 = bf16[256,128]{1,0:T(8,128)(2,1)S(1)} all-gather(bf16[16,128]{1,0:T(8,128)(2,1)S(1)} %reshape.555), channel_id=1, replica_groups=mesh['groups'=2,'rows'=16] {'rows'}, dimensions={0}, use_global_device_ids=true | all-gather | bytes 69632 | tf_op jit(solution)/shard_map/all_gather | solution.py:118
  331.9 6.1 %fusion.42 = f32[192,1,128]{2,1,0:T(1,128)S(1)} fusion(bf16[192,128,128]{2,1,0:T(8,128)(2,1)} %bitcast.276, bf16[192,128,1]{1,0,2:T(8,128)(2,1)S(1)} %bitcast.303), kind=kOutput, calls=%fused_computation.135 | convolution fusion | flops 6291456 | bytes 6438912 | tf_op jit(solution)/shard_map/tab,tb->ta/dot_general | solution.py:99
  338.0 0.9 fusion.38
  339.6 16.3 %fusion.46 = f32[16,1,2,128,1,1]{3,1,5,4,2,0:T(1,128)S(1)} fusion(f32[4,16,2,128,2,128]{5,3,0,4,2,1:T(8,128)} %get-tuple-element.176, f32[2,4,16,128,1,1]{3,0,2,1,4,5:T(2,128)S(1)} %bitcast.308), kind=kOutput, calls=%fused_computation.139 | convolution fusion | flops 50331648 | bytes 16859136 | tf_op jit(solution)/shard_map/tckilj,ltcj->kci/dot_general | solution.py:112
  355.9 36.9 %reduce-scatter.5.cloned.1.call-done = f32[16,128]{1,0:T(8,128)} async-done(((f32[256,128]{1,0:T(8,128)}), f32[16,128]{1,0:T(8,128)}) %reduce-scatter.5.cloned.1.call-update) | async-done | bytes 8208 | tf_op jit(solution)/shard_map/reduce_scatter | solution.py:102
  394.5 1.4 pad_maximum_fusion
  395.9 29.5 %psum.38 = f32[2]{0:T(128)S(1)} all-reduce(f32[2]{0:T(128)S(1)} %pad_maximum_fusion), channel_id=1, replica_groups=mesh['groups'=2,'rows'=16] {'rows'}, use_global_device_ids=true, to_apply=%region_14.15 | all-reduce | flops 2 | bytes 16 | tf_op jit(solution)/shard_map/psum | solution.py:126
  425.9 2.0 multiply_reduce_fusion
  427.9 30.1 %psum.39 = f32[]{:T(128)} all-reduce(f32[]{:T(128)} %get-tuple-element.255), channel_id=1, replica_groups=mesh['groups'=2,'rows'=16] {'rows'}, use_global_device_ids=true, to_apply=%region_16.17 | all-reduce | flops 1 | bytes 8 | tf_op jit(solution)/shard_map/psum | solution.py:129
  (509 shorter events, 75.9 us)
Async XLA Ops:
  7.2 238.3 %copy-start = (bf16[16,2,64,128]{3,2,1,0:T(8,128)(2,1)S(1)}, bf16[16,2,64,128]{3,2,1,0:T(8,128)(2,1)}, u32[]{:S(2)}) copy-start(bf16[16,2,64,128]{3,2,1,0:T(8,128)(2,1)} %param.15) | copy-start | bytes 1572868
  7.2 237.5 %reduce-scatter.3.cloned.1.call-start = ((), (), s32[]{:S(2)}) async-start(), calls=%async_computation.2 | async-start | bytes 139264 | tf_op jit(solution)/shard_map/reduce_scatter | solution.py:102
  45.6 148.0 %collective-permute-start = (f32[2,2048]{1,0:T(2,128)S(1)}, f32[2,2048]{1,0:T(2,128)S(1)}, u32[]{:S(2)}, u32[]{:S(2)}) collective-permute-start(f32[2,2048]{1,0:T(2,128)S(1)} %get-tuple-element.265), channel_id=1, source_target_pairs={{0,1},{1,2},{2,3},{3,4},{4,5},{5,6},{6,7},{7,8},{8,9},{9,10},{10,1... | collective-permute-start | bytes 49160 | tf_op jit(solution)/shard_map/ppermute | solution.py:19
  45.6 148.0 %collective-permute-start.1 = (f32[2,2048]{1,0:T(2,128)S(1)}, f32[2,2048]{1,0:T(2,128)S(1)}, u32[]{:S(2)}, u32[]{:S(2)}) collective-permute-start(f32[2,2048]{1,0:T(2,128)S(1)} %get-tuple-element.265), channel_id=1, source_target_pairs={{1,0},{2,1},{3,2},{4,3},{5,4},{6,5},{7,6},{8,7},{9,8},{10,9},{11,1... | collective-permute-start | bytes 49160 | tf_op jit(solution)/shard_map/ppermute | solution.py:21
  50.1 144.2 %collective-permute-start.2 = (f32[6,2048]{1,0:T(8,128)}, f32[6,2048]{1,0:T(8,128)S(1)}, u32[]{:S(2)}, u32[]{:S(2)}) collective-permute-start(f32[6,2048]{1,0:T(8,128)} %param.12), channel_id=1, source_target_pairs={{0,1},{1,2},{2,3},{3,4},{4,5},{5,6},{6,7},{7,8},{8,9},{9,10},{10,1... | collective-permute-start | bytes 147464 | tf_op jit(solution)/shard_map/ppermute | solution.py:19
  50.1 144.2 %collective-permute-start.3 = (f32[6,2048]{1,0:T(8,128)}, f32[6,2048]{1,0:T(8,128)S(1)}, u32[]{:S(2)}, u32[]{:S(2)}) collective-permute-start(f32[6,2048]{1,0:T(8,128)} %param.12), channel_id=1, source_target_pairs={{1,0},{2,1},{3,2},{4,3},{5,4},{6,5},{7,6},{8,7},{9,8},{10,9},{11,1... | collective-permute-start | bytes 147464 | tf_op jit(solution)/shard_map/ppermute | solution.py:21
  75.9 88.2 %copy-start.4 = (bf16[16,2,64,128]{3,2,1,0:T(8,128)(2,1)S(1)}, bf16[16,2,64,128]{3,2,1,0:T(8,128)(2,1)}, u32[]{:S(2)}) copy-start(bf16[16,2,64,128]{3,2,1,0:T(8,128)(2,1)} %param.14) | copy-start | bytes 1572868
  164.1 28.3 %copy-start.3 = (s32[4,16]{1,0:T(4,128)S(1)}, s32[4,16]{1,0:T(4,128)}, u32[]{:S(2)}) copy-start(s32[4,16]{1,0:T(4,128)} %param.17) | copy-start | bytes 772
  164.1 28.4 %copy-start.2 = (f32[6,2048]{1,0:T(8,128)S(1)}, f32[6,2048]{1,0:T(8,128)}, u32[]{:S(2)}) copy-start(f32[6,2048]{1,0:T(8,128)} %param.12) | copy-start | bytes 147460
  192.1 200.7 %reduce-scatter.5.cloned.1.call-start = ((), (), s32[]{:S(2)}) async-start(), calls=%async_computation.3 | async-start | bytes 139264 | tf_op jit(solution)/shard_map/reduce_scatter | solution.py:102
  308.5 117.4 %copy-start.1 = (f32[2,2048]{1,0:T(2,128)}, f32[2,2048]{1,0:T(2,128)S(1)}, u32[]{:S(2)}) copy-start(f32[2,2048]{1,0:T(2,128)S(1)} %get-tuple-element.259) | copy-start | bytes 49156
  308.6 30.4 %collective-permute-start.4 = (f32[2,2048]{1,0:T(2,128)S(1)}, f32[2,2048]{1,0:T(2,128)S(1)}, u32[]{:S(2)}, u32[]{:S(2)}) collective-permute-start(f32[2,2048]{1,0:T(2,128)S(1)} %get-tuple-element.259), channel_id=1, source_target_pairs={{0,1},{1,2},{2,3},{3,4},{4,5},{5,6},{6,7},{7,8},{8,9},{9,10},{10,1... | collective-permute-start | bytes 49160 | tf_op jit(solution)/shard_map/ppermute | solution.py:19
  308.6 30.3 %collective-permute-start.5 = (f32[2,2048]{1,0:T(2,128)S(1)}, f32[2,2048]{1,0:T(2,128)S(1)}, u32[]{:S(2)}, u32[]{:S(2)}) collective-permute-start(f32[2,2048]{1,0:T(2,128)S(1)} %get-tuple-element.259), channel_id=1, source_target_pairs={{1,0},{2,1},{3,2},{4,3},{5,4},{6,5},{7,6},{8,7},{9,8},{10,9},{11,1... | collective-permute-start | bytes 49160 | tf_op jit(solution)/shard_map/ppermute | solution.py:21
Sparse Core Ops, SparseCore 0:
  192.2 52.4 reduce-scatter.2
  339.0 53.7 reduce-scatter.4
where the time goes:
time: 468 us; the launch traced here: 467 us
  blocking collectives  211 us (45%)
  other arithmetic  67 us (14%)
  local copies, waits for them, and re-layouts  59 us (13%)
  matrix products  47.8 us (10%)
  waiting for transfers between devices  47.4 us (10%)
  between operations  17.1 us (4%)
  starting transfers between devices  13.7 us (3%)
    psum x2, blocking collectives, orthogonal(): length_sq = lax.psum(jnp.sum(image * image), 'rows') / entries  60.2 us
    psum x2, blocking collectives, orthogonal(): coeffs = lax.psum(local_proj, 'rows') / entries  59.6 us
    reduce_scatter x2, waiting for transfers between devices, expansions(): lax.psum_scatter(jnp.dot(selector, terms, precision=lax.Precision.HIGHEST...  47.4 us
    all_gather x2, blocking collectives, operate(): moments_all = lax.all_gather(moments, 'rows', axis=0, tiled=True)  37.1 us
    psum x1, blocking collectives, shards(): rhs_sq = lax.psum(jnp.sum(rhs * rhs), 'rows')  35.5 us
    dot_general x2, matrix products, operate(): jnp.einsum('tckilj,ltcj->kci', near_mats, neighbours, precision=lax.Preci...  32.5 us
    all_gather x1, blocking collectives, shards(): lax.all_gather(proxies, 'rows', axis=1, tiled=True)  18.9 us
    convert_element_type x32, local copies, waits for them, and re-layouts, block_group(): return mats.reshape(per_step, 2 * rank, 2 * rank).astype(jnp.bfloat16)  18.8 us
  transfers between devices with their start and end apart: 8, of which 2 were waited for; matrix products, arithmetic and copies ran while one was open for 35% of the time, Pallas kernels for 0%

commit v1 on v0

v1 whole, which is shorter than its diff:
```python
import functools

import jax
import jax.numpy as jnp
from jax import lax
from jax.experimental import pallas as pl
from jax.experimental.pallas import tpu as pltpu
from jax.sharding import PartitionSpec as P

coulomb = 1.0 / (4.0 * 3.141592653589793)
kappa = 0.5
ratio = 4.0
eps = 1e-06
MESH = pl.DeviceIdType.MESH

PROXY, NORM, MOMENT, EXPAND, DOTS = 0, 1, 2, 4, 6


def features(points):
    polar, azimuth = points[3], points[4]
    return jnp.stack(
        [
            points[0],
            points[1],
            points[2],
            jnp.sin(polar) * jnp.cos(azimuth),
            jnp.sin(polar) * jnp.sin(azimuth),
            jnp.cos(polar),
            points[5],
            jnp.zeros_like(points[0]),
        ]
    )


def pair_terms(target, source):
    tcol = lambda c: target[:, c : c + 1]
    srow = lambda c: source[c : c + 1, :]
    dx, dy, dz = tcol(0) - srow(0), tcol(1) - srow(1), tcol(2) - srow(2)
    dist_sq = dx * dx + dy * dy + dz * dz + tcol(6) + srow(6)
    inverse = lax.rsqrt(dist_sq)
    radius = dist_sq * inverse
    screen = jnp.exp(-kappa * radius)
    growth = (1.0 + kappa * radius) * screen
    single = (coulomb * srow(6)) * inverse
    cube = single * (inverse * inverse)
    double = cube * (dx * srow(3) + dy * srow(4) + dz * srow(5))
    adjoint = -cube * (dx * tcol(3) + dy * tcol(4) + dz * tcol(5))
    return single, double, adjoint, screen, growth


def total(x):
    x = jnp.sum(jnp.sum(x, axis=0), axis=0, keepdims=True)
    return jnp.broadcast_to(jnp.sum(x, axis=1, keepdims=True), x.shape)


def pack(values):
    row = lax.broadcasted_iota(jnp.int32, (16, 128), 0)
    out = jnp.zeros((16, 128), jnp.float32)
    for index, value in enumerate(values):
        out = jnp.where(row == index, value, out)
    return out


def kernel(
    n,
    near_ref,
    task_ref,
    rhs_ref,
    geo_ref,
    geo_col_ref,
    proxy_ref,
    basis_in_ref,
    basis_out_ref,
    rows_ref,
    second_ref,
    third_ref,
    hess_ref,
    wide_geo,
    all_proxy,
    near_mats,
    coupled,
    wide_u,
    mom_all,
    terms,
    exp_send,
    exp_recv,
    dots_send,
    dots_recv,
    near_out,
    far_out,
    low_exp,
    send_sem,
    recv_sem,
    halo_send,
    halo_recv,
):
    clusters = geo_ref.shape[0]
    pairs = clusters // 2
    tasks = task_ref.shape[1]
    near_count = near_ref.shape[0]
    entries = 2.0 * clusters * 128 * n
    me = lax.axis_index("rows")
    right, left = lax.rem(me + 1, n), lax.rem(me + n - 1, n)
    peer_of = lambda k: lax.rem(me + k, n)

    barrier = pltpu.get_barrier_semaphore()

    def greet(k, carry):
        pl.semaphore_signal(barrier, inc=1, device_id={"rows": peer_of(k)}, device_id_type=MESH)
        return carry

    lax.fori_loop(1, n, greet, 0)
    pl.semaphore_wait(barrier, n - 1)

    def to_all(phase, src_of, dst):
        def copy(k):
            return pltpu.make_async_remote_copy(
                src_ref=src_of(peer_of(k)),
                dst_ref=dst,
                send_sem=send_sem.at[phase, k],
                recv_sem=recv_sem.at[phase, k],
                device_id={"rows": peer_of(k)},
                device_id_type=MESH,
            )

        def start(k, carry):
            copy(k).start()
            return carry

        def wait(k, carry):
            copy(k).wait()
            return carry

        return (
            lambda: lax.fori_loop(1, n, start, 0),
            lambda: lax.fori_loop(1, n, wait, 0),
        )

    def halo(phase, src, at):
        copies = [
            pltpu.make_async_remote_copy(
                src_ref=src,
                dst_ref=at(where),
                send_sem=halo_send.at[phase, side],
                recv_sem=halo_recv.at[phase, side],
                device_id={"rows": device},
                device_id_type=MESH,
            )
            for side, (where, device) in enumerate(((0, right), (2 * clusters, left)))
        ]

        def start():
            for copy in copies:
                copy.start()

        def wait():
            for copy in copies:
                copy.wait()

        return start, wait

    def dots_phase(index):
        return to_all(DOTS - 1 + index if index else NORM, lambda p: dots_send.at[index], dots_recv.at[index, me])

    rhs = rhs_ref[...]
    message = pack([total(rhs * rhs)])
    dots_send[0] = message
    norm_start, norm_wait = dots_phase(0)
    norm_start()
    dots_recv[0, me] = message
    geo_start, geo_wait = halo(0, geo_ref, lambda where: wide_geo.at[pl.ds(where, clusters)])
    geo_start()
    wide_geo[pl.ds(clusters, clusters)] = geo_ref[...]
    proxy_start, proxy_wait = to_all(PROXY, lambda p: proxy_ref, all_proxy.at[pl.ds(me * pairs, pairs)])
    proxy_start()
    all_proxy[pl.ds(me * pairs, pairs)] = proxy_ref[...]

    lane8 = lax.broadcasted_iota(jnp.int32, (8, 128), 1)
    row8 = lax.broadcasted_iota(jnp.int32, (8, 128), 0)
    own_row = (lane8 >= 64) == (row8 == 1)

    def send_density(step):
        def moment(c, carry):
            u0 = wide_u[step, 0, pl.ds(clusters + c, 1), :]
            u1 = wide_u[step, 1, pl.ds(clusters + c, 1), :]
            low = jnp.where(row8 == 0, u0, u1).astype(jnp.bfloat16)
            got = lax.dot_general(
                low, basis_in_ref[c], (((1,), (1,)), ((), ())), preferred_element_type=jnp.float32
            )
            got = jnp.where(lane8[:1] < 64, got[0:1], got[1:2])
            mom_all[step, pl.ds(me * clusters + c, 1), :] = got.astype(jnp.bfloat16).astype(jnp.float32)
            return carry

        u_start, u_wait = halo(
            1 + step,
            wide_u.at[step, :, pl.ds(clusters, clusters)],
            lambda where: wide_u.at[step, :, pl.ds(where, clusters)],
        )
        u_start()
        for c in range(clusters):
            moment(c, 0)
        own = mom_all.at[step, pl.ds(me * clusters, clusters)]
        mom_start, mom_wait = to_all(MOMENT + step, lambda p: own, own)
        mom_start()
        return u_wait, mom_wait

    def apply(step, u_wait, mom_wait):
        mom_wait()

        def far_terms(group, carry):
            for q in range(8):
                t = group * 8 + q
                picked = mom_all[step, pl.ds(task_ref[1, t], 1), :]
                low = jnp.broadcast_to(picked, (8, 128)).astype(jnp.bfloat16)
                got = lax.dot_general(
                    low, coupled[t], (((1,), (1,)), ((), ())), preferred_element_type=jnp.float32
                )
                terms[pl.ds(t, 1), :] = got[0:1]
            return carry

        lax.fori_loop(0, tasks // 8, far_terms, 0)
        term = terms[...]
        high = term.astype(jnp.bfloat16)
        rest = term - high.astype(jnp.float32)
        mid = rest.astype(jnp.bfloat16)
        low = (rest - mid.astype(jnp.float32)).astype(jnp.bfloat16)
        task_rows = rows_ref[0:1, :]
        width = task_rows.shape[1]

        def choose(block, carry):
            start = pl.multiple_of(block * 128, 128)
            wanted = start + lax.broadcasted_iota(jnp.int32, (128, width), 0)
            selector = jnp.where(task_rows == wanted, 1.0, 0.0).astype(jnp.bfloat16)
            dot = lambda part: jnp.dot(selector, part, preferred_element_type=jnp.float32)
            exp_send[step, pl.ds(start, 128), :] = dot(high) + (dot(mid) + dot(low))
            return carry

        lax.fori_loop(0, n * clusters // 128, choose, 0)
        exp_start, exp_wait = to_all(
            EXPAND + step,
            lambda p: exp_send.at[step, pl.ds(p * clusters, clusters)],
            exp_recv.at[step, me],
        )
        exp_start()
        exp_recv[step, me] = exp_send[step, pl.ds(me * clusters, clusters), :]
        u_wait()

        def near_apply(r, carry):
            acc = [jnp.zeros((128, 128), jnp.float32) for _ in range(2)]
            for t in range(near_count):
                b = near_ref[t, r]
                u0 = wide_u[step, 0, pl.ds(b, 1), :]
                u1 = wide_u[step, 1, pl.ds(b, 1), :]
                for k in range(2):
                    acc[k] = acc[k] + (
                        near_mats[r * near_count + t, k, :, 0:128] * u0
                        + near_mats[r * near_count + t, k, :, 128:256] * u1
                    )
            for k in range(2):
                near_out[k, pl.ds(r, 1), :] = jnp.sum(jnp.transpose(acc[k]), axis=0, keepdims=True)
            return carry

        lax.fori_loop(0, clusters, near_apply, 0)
        exp_wait()
        low_exp[...] = jnp.sum(exp_recv[step], axis=0)
        for c in range(clusters):
            row = jnp.where(own_row & (row8 < 2), low_exp[pl.ds(c, 1), :], 0.0).astype(jnp.bfloat16)
            got = jnp.dot(row, basis_out_ref[c], preferred_element_type=jnp.float32)
            far_out[0, pl.ds(c, 1), :] = got[0:1]
            far_out[1, pl.ds(c, 1), :] = got[1:2]
        u = wide_u[step, :, pl.ds(clusters, clusters), :]
        which = lax.broadcasted_iota(jnp.int32, u.shape, 0)
        diag = jnp.where(which == 0, (1.0 + ratio) / 2.0, (1.0 + 1.0 / ratio) / 2.0)
        return diag * u + near_out[...] + far_out[...]

    def safe(top, bottom):
        return jnp.where(bottom > 0.0, top / jnp.where(bottom > 0.0, bottom, 1.0), 0.0)

    def exchange(index, values):
        message = pack(values)
        dots_send[index] = message
        start, wait = dots_phase(index)
        start()
        dots_recv[index, me] = message
        wait()
        return [dots_recv[index, :, q, :] for q in range(len(values))]

    add = lambda x: jnp.sum(x, axis=0, keepdims=True)

    norm_wait()
    rhs_sq = add(dots_recv[0, :, 0, :])
    first = rhs / jnp.sqrt(rhs_sq / entries + eps)
    wide_u[0, :, pl.ds(clusters, clusters), :] = first
    u_wait, mom_wait = send_density(0)

    geo_wait()

    def near_build(r, carry):
        for t in range(near_count):
            source = wide_geo[near_ref[t, r]]
            for lo in range(0, 128, 32):
                single, double, adjoint, screen, growth = pair_terms(geo_col_ref[r, lo : lo + 32, :], source)
                at = r * near_count + t
                near_mats[at, 0, lo : lo + 32, 0:128] = double - double * (ratio * growth)
                near_mats[at, 0, lo : lo + 32, 128:256] = single * screen - single
                near_mats[at, 1, lo : lo + 32, 0:128] = adjoint - adjoint * growth
                near_mats[at, 1, lo : lo + 32, 128:256] = adjoint - adjoint * (growth / ratio)
        return carry

    lax.fori_loop(0, clusters, near_build, 0)

    proxy_wait()
    terms[...] = jnp.zeros_like(terms)
    upper = lane8 >= 64
    part = jnp.where(upper[:1], 1.0 / ratio, 1.0)

    def cluster_points(c):
        both = all_proxy[lax.div(c, 2)]
        return jnp.where(upper.astype(jnp.int32) == lax.rem(c, 2), both, pltpu.roll(both, 64, 1))

    def far_build(group, carry):
        for q in range(2):
            t = group * 2 + q
            target = jnp.transpose(cluster_points(task_ref[0, t]))
            source = cluster_points(task_ref[1, t])
            for lo in range(0, 64, 32):
                single, double, adjoint, screen, growth = pair_terms(target[lo : lo + 32], source)
                top = jnp.where(
                    upper[:1], single * screen - single, double - double * (ratio * growth)
                )
                bottom = adjoint - adjoint * (growth * part)
                coupled[t, lo : lo + 32, :] = top.astype(jnp.bfloat16)
                coupled[t, 64 + lo : 96 + lo, :] = bottom.astype(jnp.bfloat16)
        return carry

    lax.fori_loop(0, tasks // 2, far_build, 0)

    image = apply(0, u_wait, mom_wait)
    ff, fw = total(first * first), total(first * image)
    c1 = safe(fw, ff)
    left_over = image - c1 * first
    ff, fw, c1, rr, fr = exchange(1, [ff, fw, c1, total(left_over * left_over), total(first * left_over)])
    h11 = add(fw) / entries
    d1 = c1 - h11
    h21 = jnp.sqrt(jnp.maximum(add(rr + 2.0 * d1 * fr + d1 * d1 * ff), 0.0) / entries + eps)
    second = (image - h11 * first) / h21
    second_ref[...] = second
    wide_u[1, :, pl.ds(clusters, clusters), :] = second
    u_wait, mom_wait = send_density(1)

    image = apply(1, u_wait, mom_wait)
    ff, fv, vv = total(first * first), total(first * second), total(second * second)
    fw, vw = total(first * image), total(second * image)
    c1 = safe(fw, ff)
    left_over = image - c1 * first
    c2 = safe(total(second * left_over), vv)
    left_over = left_over - c2 * second
    ff, fv, vv, fw, vw, c1, c2, rr, fr, vr = exchange(
        2,
        [ff, fv, vv, fw, vw, c1, c2]
        + [total(x * left_over) for x in (left_over, first, second)],
    )
    h12, h22 = add(fw) / entries, add(vw) / entries
    d1, d2 = c1 - h12, c2 - h22
    length_sq = add(rr + 2.0 * (d1 * fr + d2 * vr) + d1 * d1 * ff + 2.0 * d1 * d2 * fv + d2 * d2 * vv)
    h32 = jnp.sqrt(jnp.maximum(length_sq, 0.0) / entries + eps)
    third_ref[...] = (image - h12 * first - h22 * second) / h32
    out = jnp.zeros((8, 128), jnp.float32)
    for index, value in enumerate((h11, h21, h12, h22, h32)):
        out = jnp.where(lane8 == index, value, out)
    hess_ref[...] = out


def shards(rhs, geometry, proxies, basis_in, basis_out, far_tasks, near_tiles):
    clusters = basis_in.shape[0]
    rank = basis_in.shape[2]
    panels = geometry.shape[1]
    members = panels // clusters
    n = lax.axis_size("rows")
    total_clusters = clusters * n
    first_cluster = lax.axis_index("rows") * clusters
    near_local = (near_tiles - first_cluster + clusters) % total_clusters
    near_count = near_tiles.shape[0]
    tasks = far_tasks.shape[1]
    width = -(-tasks // 128) * 128

    geo = features(geometry).reshape(8, clusters, members)
    geo_row = jnp.transpose(geo, (1, 0, 2))
    geo_col = jnp.transpose(geo, (1, 2, 0))
    proxy = jnp.transpose(features(proxies).reshape(8, clusters // 2, 2 * rank), (1, 0, 2))
    task_rows = jnp.pad(far_tasks[0:1], ((0, 7), (0, width - tasks)), constant_values=-1)

    f32, bf16 = jnp.float32, jnp.bfloat16
    vmem = pl.BlockSpec(memory_space=pltpu.VMEM)
    smem = pl.BlockSpec(memory_space=pltpu.SMEM)
    second, third, hess = pl.pallas_call(
        functools.partial(kernel, n),
        out_shape=(
            jax.ShapeDtypeStruct((2, clusters, members), f32),
            jax.ShapeDtypeStruct((2, clusters, members), f32),
            jax.ShapeDtypeStruct((8, 128), f32),
        ),
        in_specs=[smem, smem] + [vmem] * 7,
        out_specs=(vmem, vmem, vmem),
        scratch_shapes=[
            pltpu.VMEM((3 * clusters, 8, members), f32),
            pltpu.VMEM((total_clusters // 2, 8, 2 * rank), f32),
            pltpu.VMEM((clusters * near_count, 2, members, 2 * members), f32),
            pltpu.VMEM((tasks, 2 * rank, 2 * rank), bf16),
            pltpu.VMEM((2, 2, 3 * clusters, members), f32),
            pltpu.VMEM((2, total_clusters, 2 * rank), f32),
            pltpu.VMEM((width, 2 * rank), f32),
            pltpu.VMEM((2, total_clusters, 2 * rank), f32),
            pltpu.VMEM((2, n, clusters, 2 * rank), f32),
            pltpu.VMEM((3, 16, 128), f32),
            pltpu.VMEM((3, n, 16, 128), f32),
            pltpu.VMEM((2, clusters, members), f32),
            pltpu.VMEM((2, clusters, members), f32),
            pltpu.VMEM((clusters, 2 * rank), f32),
            pltpu.SemaphoreType.DMA((8, n)),
            pltpu.SemaphoreType.DMA((8, n)),
            pltpu.SemaphoreType.DMA((3, 2)),
            pltpu.SemaphoreType.DMA((3, 2)),
        ],
        compiler_params=pltpu.CompilerParams(
            collective_id=0, has_side_effects=True, vmem_limit_bytes=48 * 1024 * 1024
        ),
    )(
        near_local,
        far_tasks,
        rhs.reshape(2, clusters, members),
        geo_row,
        geo_col,
        proxy,
        basis_in.reshape(clusters, 2 * rank, members),
        basis_out.reshape(clusters, 2 * rank, members),
        task_rows,
    )
    return (second.reshape(2, panels), third.reshape(2, panels), hess[0, :5])


def solution(mesh):
    return jax.shard_map(
        shards,
        mesh=mesh,
        in_specs=(
            P(None, ("groups", "rows")),
            P(None, ("groups", "rows")),
            P(None, ("groups", "rows")),
            P(("groups", "rows"), None, None, None),
            P(("groups", "rows"), None, None, None),
            P(None, ("groups", "rows")),
            P(None, ("groups", "rows")),
        ),
        out_specs=(P(None, ("groups", "rows")), P(None, ("groups", "rows")), P("groups")),
        check_vma=False,
    )
```

time: 468 us -> 115 us (0.25)
  blocking collectives: 211 us -> 0 us
  Pallas kernels: 0 us -> 107 us
  other arithmetic: 67 us -> 1.69 us
  local copies, waits for them, and re-layouts: 59 us -> 5.85 us
  matrix products: 47.8 us -> 0 us
  waiting for transfers between devices: 47.4 us -> 0 us
  between operations: 17.1 us -> 0.77 us
  starting transfers between devices: 13.7 us -> 0 us
    psum x5 -> x0, blocking collectives: 155 us -> none  [the longest x2 60.2 us: orthogonal(): length_sq = lax.psum(jnp.sum(image * image), 'rows') / entries]
    pallas_call x0 -> x1, Pallas kernels: none -> 107 us  [shards(): pl.pallas_call(functools.partial(kernel, n), out_shape=(jax.ShapeDtypeStr...]
    all_gather x3 -> x0, blocking collectives: 56.1 us -> none  [the longest x2 37.1 us: operate(): moments_all = lax.all_gather(moments, 'rows', axis=0, tiled=True)]
    dot_general x10 -> x0, matrix products: 47.8 us -> none  [the longest x2 32.5 us: operate(): jnp.einsum('tckilj,ltcj->kci', near_mats, neighbours, precision=lax.Preci...]
    reduce_scatter x2 -> x0, waiting for transfers between devices: 47.4 us -> none  [expansions(): lax.psum_scatter(jnp.dot(selector, terms, precision=lax.Precision.HIGHEST...]
    gather x41 -> x0, local copies, waits for them, and re-layouts: 24.3 us -> none  [the longest x16 9.27 us: block_group(): all_proxy[:, b]]
    another operation x54 -> x1, other arithmetic: 23.3 us -> 0.25 us  [features(): jnp.stack([points[0], points[1], points[2], jnp.sin(polar) * jnp.cos(azim...]
    convert_element_type x32 -> x0, local copies, waits for them, and re-layouts: 18.8 us -> none  [block_group(): return mats.reshape(per_step, 2 * rank, 2 * rank).astype(jnp.bfloat16)]
  transfers between devices with their start and end apart: 8 -> 0, of which waited for: 2 -> 0; matrix products, arithmetic and copies ran while one was open for 35% -> 0% of each run, Pallas kernels for 0% -> 0%
where the time goes in v1:
time: 115 us
  Pallas kernels  107 us (93%)
  local copies, waits for them, and re-layouts  5.85 us (5%)
  other arithmetic  1.69 us (1%)
    pallas_call x1, Pallas kernels, shards(): pl.pallas_call(functools.partial(kernel, n), out_shape=(jax.ShapeDtypeStr...  107 us
    unnamed x19, local copies, waits for them, and re-layouts  3.61 us

profile of v1, /device:TPU:0, one launch (start us, length us, event | category | flops | bytes accessed | tf_op | source)
XLA Modules:
  0.0 115.0 jit_solution(16331396431205699576)
XLA Ops:
  0.6 1.4 %fusion.1 = (f32[1,2048]{1,0:T(1,128)S(1)}, f32[1,2048]{1,0:T(1,128)S(1)}, f32[1,2048]{1,0:T(1,128)S(1)}, f32[1,2048]{1,0:T(1,128)S(1)}) fusion(f32[6,2048]{1,0:T(8,128)} %param.8), kind=kLoop, calls=%fused_computation.26 | loop fusion | flops 4096 | bytes 57344 | tf_op jit(solution)/shard_map/slice | solution.py:29
  2.1 0.8 slice_bitcast_fusion
  3.0 0.0 copy-start
  3.0 0.0 copy-start.1
  3.0 0.3 copy.19
  3.3 0.0 copy-start.3
  3.4 0.7 copy-done.3
  4.1 0.2 slice_bitcast_fusion.2
  4.4 0.0 copy-start.4
  4.4 0.1 stack.45
  4.4 0.7 copy-done.4
  5.1 0.0 slice-start
  5.1 0.7 slice-done
  5.8 0.0 copy-start.5
  5.8 0.7 copy-done.5
  6.5 0.0 copy-start.2
  6.5 0.0 copy-done
  6.5 0.0 copy-done.1
  6.5 0.7 copy-done.2
  7.2 106.7 %shard_map.94 = (f32[2,16,128]{2,1,0:T(8,128)S(1)}, f32[2,16,128]{2,1,0:T(8,128)S(1)}, f32[8,128]{1,0:T(8,128)S(1)}) custom-call(s32[4,16]{1,0:T(4,128)S(1)} %add_select_fusion.near_ref, s32[2,192]{1,0:T(2,128)S(1)} %copy-done.2, f32[2,16,128]{2,1,0:T(8,128)S(1)} %bitcast.42, f32[16,8,128]{2,1,0:T(8,128)S(1)} %bitcast.40, f32[16,128,8]{2,1,0:T(8,128)S(1)} %bitcast.37, ...), custom_call_target="tpu_custom_call" | custom-call | tf_op jit(solution)/shard_map/pallas_call | solution.py:396
  113.9 0.6 copy_bitcast_fusion.1
  114.5 0.5 slice_bitcast_fusion.3
  (12 shorter events, 0.1 us)
Async XLA Ops:
  3.0 3.5 %copy-start = (bf16[16,2,64,128]{3,2,1,0:T(8,128)(2,1)S(1)}, bf16[16,2,64,128]{3,2,1,0:T(8,128)(2,1)}, u32[]{:S(2)}) copy-start(bf16[16,2,64,128]{3,2,1,0:T(8,128)(2,1)} %param.10) | copy-start | bytes 1572868
  3.0 3.5 %copy-start.1 = (bf16[16,2,64,128]{3,2,1,0:T(8,128)(2,1)S(1)}, bf16[16,2,64,128]{3,2,1,0:T(8,128)(2,1)}, u32[]{:S(2)}) copy-start(bf16[16,2,64,128]{3,2,1,0:T(8,128)(2,1)} %param.11) | copy-start | bytes 1572868
  3.3 0.8 copy-start.3
  4.4 0.7 copy-start.4
  5.1 0.7 slice-start
  5.8 0.7 copy-start.5
  6.5 0.7 copy-start.2

commit v2 on v1

--- a/solution.py
+++ b/solution.py
@@ -12,6 +12,12 @@
 ratio = 4.0
 eps = 1e-06
 MESH = pl.DeviceIdType.MESH
+
+FAR_UNROLL = 4
+FAR_CHUNK = 32
+NEAR_CHUNK = 32
+TERM_UNROLL = 16
+UNROLL = 1
 
 PROXY, NORM, MOMENT, EXPAND, DOTS = 0, 1, 2, 4, 6
 
@@ -33,18 +39,16 @@
 
 
 def pair_terms(target, source):
-    tcol = lambda c: target[:, c : c + 1]
-    srow = lambda c: source[c : c + 1, :]
-    dx, dy, dz = tcol(0) - srow(0), tcol(1) - srow(1), tcol(2) - srow(2)
-    dist_sq = dx * dx + dy * dy + dz * dz + tcol(6) + srow(6)
+    dx, dy, dz = target[0] - source[0], target[1] - source[1], target[2] - source[2]
+    dist_sq = dx * dx + dy * dy + dz * dz + target[6] + source[6]
     inverse = lax.rsqrt(dist_sq)
     radius = dist_sq * inverse
     screen = jnp.exp(-kappa * radius)
     growth = (1.0 + kappa * radius) * screen
-    single = (coulomb * srow(6)) * inverse
+    single = (coulomb * source[6]) * inverse
     cube = single * (inverse * inverse)
-    double = cube * (dx * srow(3) + dy * srow(4) + dz * srow(5))
-    adjoint = -cube * (dx * tcol(3) + dy * tcol(4) + dz * tcol(5))
+    double = cube * (dx * source[3] + dy * source[4] + dz * source[5])
+    adjoint = -cube * (dx * target[3] + dy * target[4] + dz * target[5])
     return single, double, adjoint, screen, growth
 
 
@@ -88,7 +92,9 @@
     dots_recv,
     near_out,
     far_out,
+    pair_out,
     low_exp,
+    spreader,
     send_sem,
     recv_sem,
     halo_send,
@@ -97,6 +103,7 @@
     clusters = geo_ref.shape[0]
     pairs = clusters // 2
     tasks = task_ref.shape[1]
+    half = tasks // 2
     near_count = near_ref.shape[0]
     entries = 2.0 * clusters * 128 * n
     me = lax.axis_index("rows")
@@ -132,8 +139,8 @@
             return carry
 
         return (
-            lambda: lax.fori_loop(1, n, start, 0),
-            lambda: lax.fori_loop(1, n, wait, 0),
+            lambda: lax.fori_loop(1, n, start, 0, unroll=UNROLL),
+            lambda: lax.fori_loop(1, n, wait, 0, unroll=UNROLL),
         )
 
     def halo(phase, src, at):
@@ -177,6 +184,7 @@
 
     lane8 = lax.broadcasted_iota(jnp.int32, (8, 128), 1)
     row8 = lax.broadcasted_iota(jnp.int32, (8, 128), 0)
+    upper = lane8 >= 64
     own_row = (lane8 >= 64) == (row8 == 1)
 
     def send_density(step):
@@ -208,17 +216,22 @@
         mom_wait()
 
         def far_terms(group, carry):
-            for q in range(8):
-                t = group * 8 + q
-                picked = mom_all[step, pl.ds(task_ref[1, t], 1), :]
-                low = jnp.broadcast_to(picked, (8, 128)).astype(jnp.bfloat16)
-                got = lax.dot_general(
-                    low, coupled[t], (((1,), (1,)), ((), ())), preferred_element_type=jnp.float32
-                )
-                terms[pl.ds(t, 1), :] = got[0:1]
-            return carry
-
-        lax.fori_loop(0, tasks // 8, far_terms, 0)
+            for q in range(TERM_UNROLL):
+                p = group * TERM_UNROLL + q
+                picked_a = mom_all[step, pl.ds(task_ref[1, p], 1), :]
+                picked_b = mom_all[step, pl.ds(task_ref[1, half + p], 1), :]
+                low = jnp.where(row8 == 0, picked_a, picked_b).astype(jnp.bfloat16)
+                got = jnp.dot(low, coupled[p], preferred_element_type=jnp.float32)
+                for k in range(2):
+                    block = got[:, k * 128 : k * 128 + 128]
+                    pair_out[k, pl.ds(p, 1), :] = jnp.where(upper[:1], block[1:2], block[0:1])
+            return carry
+
+        lax.fori_loop(0, half // TERM_UNROLL, far_terms, 0)
+        out0, out1 = pair_out[0], pair_out[1]
+        below = lax.broadcasted_iota(jnp.int32, out0.shape, 1) < 64
+        terms[0:half, :] = jnp.where(below, out0, pltpu.roll(out1, 64, 1))
+        terms[half:tasks, :] = jnp.where(below, pltpu.roll(out0, 64, 1), out1)
         term = terms[...]
         high = term.astype(jnp.bfloat16)
         rest = term - high.astype(jnp.float32)
@@ -287,53 +300,72 @@
 
     add = lambda x: jnp.sum(x, axis=0, keepdims=True)
 
+    geo_wait()
+
+    def near_build(r, carry):
+        sources = [wide_geo[near_ref[t, r]] for t in range(near_count)]
+        for lo in range(0, 128, NEAR_CHUNK):
+            hi = lo + NEAR_CHUNK
+            tcol = [
+                jnp.broadcast_to(geo_col_ref[r, lo:hi, c : c + 1], (NEAR_CHUNK, 128)) for c in range(7)
+            ]
+            for t in range(near_count):
+                srow = [sources[t][c : c + 1, :] for c in range(7)]
+                single, double, adjoint, screen, growth = pair_terms(tcol, srow)
+                at = r * near_count + t
+                near_mats[at, 0, lo:hi, 0:128] = double - double * (ratio * growth)
+                near_mats[at, 0, lo:hi, 128:256] = single * screen - single
+                near_mats[at, 1, lo:hi, 0:128] = adjoint - adjoint * growth
+                near_mats[at, 1, lo:hi, 128:256] = adjoint - adjoint * (growth / ratio)
+        return carry
+
+    lax.fori_loop(0, clusters, near_build, 0)
+
     norm_wait()
     rhs_sq = add(dots_recv[0, :, 0, :])
     first = rhs / jnp.sqrt(rhs_sq / entries + eps)
     wide_u[0, :, pl.ds(clusters, clusters), :] = first
     u_wait, mom_wait = send_density(0)
 
-    geo_wait()
-
-    def near_build(r, carry):
-        for t in range(near_count):
-            source = wide_geo[near_ref[t, r]]
-            for lo in range(0, 128, 32):
-                single, double, adjoint, screen, growth = pair_terms(geo_col_ref[r, lo : lo + 32, :], source)
-                at = r * near_count + t
-                near_mats[at, 0, lo : lo + 32, 0:128] = double - double * (ratio * growth)
-                near_mats[at, 0, lo : lo + 32, 128:256] = single * screen - single
-                near_mats[at, 1, lo : lo + 32, 0:128] = adjoint - adjoint * growth
-                near_mats[at, 1, lo : lo + 32, 128:256] = adjoint - adjoint * (growth / ratio)
-        return carry
-
-    lax.fori_loop(0, clusters, near_build, 0)
-
     proxy_wait()
     terms[...] = jnp.zeros_like(terms)
-    upper = lane8 >= 64
-    part = jnp.where(upper[:1], 1.0 / ratio, 1.0)
-
-    def cluster_points(c):
+    row = lax.broadcasted_iota(jnp.int32, spreader.shape, 0)
+    lane = lax.broadcasted_iota(jnp.int32, spreader.shape, 1)
+    same = (row % 8 == lane // 128) & (row // 24 == (lane % 128) // 64)
+    spreader[...] = jnp.where(same, 1.0, 0.0).astype(jnp.bfloat16)
+
+    def cluster(c):
         both = all_proxy[lax.div(c, 2)]
-        return jnp.where(upper.astype(jnp.int32) == lax.rem(c, 2), both, pltpu.roll(both, 64, 1))
+        return jnp.where(lax.rem(c, 2) == 0, both, pltpu.roll(both, 64, 1))
+
+    def split(x):
+        high = x.astype(jnp.bfloat16).astype(jnp.float32)
+        mid = (x - high).astype(jnp.bfloat16).astype(jnp.float32)
+        return [high, mid, x - high - mid]
 
     def far_build(group, carry):
-        for q in range(2):
-            t = group * 2 + q
-            target = jnp.transpose(cluster_points(task_ref[0, t]))
-            source = cluster_points(task_ref[1, t])
-            for lo in range(0, 64, 32):
-                single, double, adjoint, screen, growth = pair_terms(target[lo : lo + 32], source)
-                top = jnp.where(
-                    upper[:1], single * screen - single, double - double * (ratio * growth)
-                )
-                bottom = adjoint - adjoint * (growth * part)
-                coupled[t, lo : lo + 32, :] = top.astype(jnp.bfloat16)
-                coupled[t, 64 + lo : 96 + lo, :] = bottom.astype(jnp.bfloat16)
+        for q in range(FAR_UNROLL):
+            p = group * FAR_UNROLL + q
+            target = jnp.where(
+                upper, pltpu.roll(cluster(task_ref[0, half + p]), 64, 1), cluster(task_ref[0, p])
+            )
+            parts = split(cluster(task_ref[1, p])) + split(cluster(task_ref[1, half + p]))
+            parts = jnp.transpose(jnp.concatenate(parts, axis=0))[0:64].astype(jnp.bfloat16)
+            spread = jnp.dot(parts, spreader[...], preferred_element_type=jnp.float32)
+            trow = [target[c : c + 1, :] for c in range(7)]
+            for lo in range(0, 64, FAR_CHUNK):
+                hi = lo + FAR_CHUNK
+                scol = [spread[lo:hi, c * 128 : c * 128 + 128] for c in range(7)]
+                single, double, adjoint, screen, growth = pair_terms(trow, scol)
+                coupled[p, lo:hi, 0:128] = (double - double * (ratio * growth)).astype(jnp.bfloat16)
+                coupled[p, 64 + lo : 64 + hi, 0:128] = (single * screen - single).astype(jnp.bfloat16)
+                coupled[p, lo:hi, 128:256] = (adjoint - adjoint * growth).astype(jnp.bfloat16)
+                coupled[p, 64 + lo : 64 + hi, 128:256] = (
+                    adjoint - adjoint * (growth / ratio)
+                ).astype(jnp.bfloat16)
         return carry
 
-    lax.fori_loop(0, tasks // 2, far_build, 0)
+    lax.fori_loop(0, half // FAR_UNROLL, far_build, 0)
 
     image = apply(0, u_wait, mom_wait)
     ff, fw = total(first * first), total(first * image)
@@ -406,7 +438,7 @@
             pltpu.VMEM((3 * clusters, 8, members), f32),
             pltpu.VMEM((total_clusters // 2, 8, 2 * rank), f32),
             pltpu.VMEM((clusters * near_count, 2, members, 2 * members), f32),
-            pltpu.VMEM((tasks, 2 * rank, 2 * rank), bf16),
+            pltpu.VMEM((tasks // 2, 2 * rank, 4 * rank), bf16),
             pltpu.VMEM((2, 2, 3 * clusters, members), f32),
             pltpu.VMEM((2, total_clusters, 2 * rank), f32),
             pltpu.VMEM((width, 2 * rank), f32),
@@ -416,7 +448,9 @@
             pltpu.VMEM((3, n, 16, 128), f32),
             pltpu.VMEM((2, clusters, members), f32),
             pltpu.VMEM((2, clusters, members), f32),
+            pltpu.VMEM((2, tasks // 2, 2 * rank), f32),
             pltpu.VMEM((clusters, 2 * rank), f32),
+            pltpu.VMEM((48, 896), bf16),
             pltpu.SemaphoreType.DMA((8, n)),
             pltpu.SemaphoreType.DMA((8, n)),
             pltpu.SemaphoreType.DMA((3, 2)),

time: 115 us -> 79.3 us (0.69)
  Pallas kernels: 107 us -> 70.7 us
    pallas_call x1, Pallas kernels: 107 us -> 70.7 us  [shards(): pl.pallas_call(functools.partial(kernel, n), out_shape=(jax.ShapeDtypeStr...]
where the time goes in v2:
time: 79.3 us; the launch traced here: 79 us
  Pallas kernels  70.7 us (89%)
  local copies, waits for them, and re-layouts  5.85 us (7%)
  other arithmetic  1.69 us (2%)
    pallas_call x1, Pallas kernels, shards(): pl.pallas_call(functools.partial(kernel, n), out_shape=(jax.ShapeDtypeStr...  70.7 us
    unnamed x19, local copies, waits for them, and re-layouts  3.61 us

profile of v2, /device:TPU:0, one launch (start us, length us, event | category | flops | bytes accessed | tf_op | source)
XLA Modules:
  0.0 79.0 jit_solution(11270357916055316414)
XLA Ops:
  0.6 1.4 %fusion.1 = (f32[1,2048]{1,0:T(1,128)S(1)}, f32[1,2048]{1,0:T(1,128)S(1)}, f32[1,2048]{1,0:T(1,128)S(1)}, f32[1,2048]{1,0:T(1,128)S(1)}) fusion(f32[6,2048]{1,0:T(8,128)} %param.8), kind=kLoop, calls=%fused_computation.26 | loop fusion | flops 4096 | bytes 57344 | tf_op jit(solution)/shard_map/slice | solution.py:35
  2.1 0.8 %slice_bitcast_fusion = f32[1,3,16,128]{3,1,2,0:T(4,128)S(1)} fusion(f32[6,2048]{1,0:T(8,128)} %param.8), kind=kLoop, calls=%fused_computation.1 | loop fusion | bytes 49152
  3.0 0.0 copy-start
  3.0 0.0 copy-start.1
  3.0 0.3 copy.19
  3.3 0.0 copy-start.3
  3.4 0.7 copy-done.3
  4.1 0.2 slice_bitcast_fusion.2
  4.4 0.0 copy-start.4
  4.4 0.1 stack.45
  4.4 0.7 copy-done.4
  5.1 0.0 slice-start
  5.1 0.7 slice-done
  5.8 0.0 copy-start.5
  5.8 0.7 copy-done.5
  6.5 0.0 copy-start.2
  6.5 0.0 copy-done
  6.5 0.0 copy-done.1
  6.5 0.7 copy-done.2
  7.2 70.7 %shard_map.94 = (f32[2,16,128]{2,1,0:T(8,128)S(1)}, f32[2,16,128]{2,1,0:T(8,128)S(1)}, f32[8,128]{1,0:T(8,128)S(1)}) custom-call(s32[4,16]{1,0:T(4,128)S(1)} %add_select_fusion.near_ref, s32[2,192]{1,0:T(2,128)S(1)} %copy-done.2, f32[2,16,128]{2,1,0:T(8,128)S(1)} %bitcast.42, f32[16,8,128]{2,1,0:T(8,128)S(1)} %bitcast.40, f32[16,128,8]{2,1,0:T(8,128)S(1)} %bitcast.37, ...), custom_call_target="tpu_custom_call" | custom-call | tf_op jit(solution)/shard_map/pallas_call | solution.py:428
  77.8 0.6 copy_bitcast_fusion.1
  78.5 0.5 slice_bitcast_fusion.3
  (12 shorter events, 0.1 us)
Async XLA Ops:
  3.0 3.5 %copy-start = (bf16[16,2,64,128]{3,2,1,0:T(8,128)(2,1)S(1)}, bf16[16,2,64,128]{3,2,1,0:T(8,128)(2,1)}, u32[]{:S(2)}) copy-start(bf16[16,2,64,128]{3,2,1,0:T(8,128)(2,1)} %param.10) | copy-start | bytes 1572868
  3.0 3.5 %copy-start.1 = (bf16[16,2,64,128]{3,2,1,0:T(8,128)(2,1)S(1)}, bf16[16,2,64,128]{3,2,1,0:T(8,128)(2,1)}, u32[]{:S(2)}) copy-start(bf16[16,2,64,128]{3,2,1,0:T(8,128)(2,1)} %param.11) | copy-start | bytes 1572868
  3.3 0.8 copy-start.3
  4.4 0.7 copy-start.4
  5.1 0.7 slice-start
  5.8 0.7 copy-start.5
  6.5 0.7 copy-start.2

commit v3 on v2

--- a/solution.py
+++ b/solution.py
@@ -13,7 +13,7 @@
 eps = 1e-06
 MESH = pl.DeviceIdType.MESH
 
-FAR_UNROLL = 4
+FAR_UNROLL = 8
 FAR_CHUNK = 32
 NEAR_CHUNK = 32
 TERM_UNROLL = 16
@@ -58,10 +58,10 @@
 
 
 def pack(values):
-    row = lax.broadcasted_iota(jnp.int32, (16, 128), 0)
-    out = jnp.zeros((16, 128), jnp.float32)
+    lane = lax.broadcasted_iota(jnp.int32, (1, 128), 1)
+    out = jnp.zeros((1, 128), jnp.float32)
     for index, value in enumerate(values):
-        out = jnp.where(row == index, value, out)
+        out = jnp.where(lane == index, value, out)
     return out
 
 
@@ -71,10 +71,10 @@
     task_ref,
     rhs_ref,
     geo_ref,
-    geo_col_ref,
+    geo_col_hbm,
     proxy_ref,
-    basis_in_ref,
-    basis_out_ref,
+    basis_in_hbm,
+    basis_out_hbm,
     rows_ref,
     second_ref,
     third_ref,
@@ -84,6 +84,7 @@
     near_mats,
     coupled,
     wide_u,
+    mom_bf,
     mom_all,
     terms,
     exp_send,
@@ -94,7 +95,12 @@
     far_out,
     pair_out,
     low_exp,
+    dots_flat,
     spreader,
+    geo_col_ref,
+    basis_in_ref,
+    basis_out_ref,
+    load_sem,
     send_sem,
     recv_sem,
     halo_send,
@@ -110,6 +116,19 @@
     right, left = lax.rem(me + 1, n), lax.rem(me + n - 1, n)
     peer_of = lambda k: lax.rem(me + k, n)
 
+    loads = [
+        pltpu.make_async_copy(src, dst, load_sem.at[i])
+        for i, (src, dst) in enumerate(
+            (
+                (geo_col_hbm, geo_col_ref),
+                (basis_in_hbm, basis_in_ref),
+                (basis_out_hbm, basis_out_ref),
+            )
+        )
+    ]
+    for load in loads:
+        load.start()
+
     barrier = pltpu.get_barrier_semaphore()
 
     def greet(k, carry):
@@ -170,7 +189,7 @@
         return to_all(DOTS - 1 + index if index else NORM, lambda p: dots_send.at[index], dots_recv.at[index, me])
 
     rhs = rhs_ref[...]
-    message = pack([total(rhs * rhs)])
+    message = total(rhs * rhs)
     dots_send[0] = message
     norm_start, norm_wait = dots_phase(0)
     norm_start()
@@ -178,8 +197,41 @@
     geo_start, geo_wait = halo(0, geo_ref, lambda where: wide_geo.at[pl.ds(where, clusters)])
     geo_start()
     wide_geo[pl.ds(clusters, clusters)] = geo_ref[...]
-    proxy_start, proxy_wait = to_all(PROXY, lambda p: proxy_ref, all_proxy.at[pl.ds(me * pairs, pairs)])
-    proxy_start()
+    twin = me + 1 - 2 * lax.rem(me, 2)
+
+    def proxy_copy(src, owner, sem, device):
+        return pltpu.make_async_remote_copy(
+            src_ref=src,
+            dst_ref=all_proxy.at[pl.ds(owner * pairs, pairs)],
+            send_sem=send_sem.at[PROXY, sem],
+            recv_sem=recv_sem.at[PROXY, sem],
+            device_id={"rows": device},
+            device_id_type=MESH,
+        )
+
+    def proxy_far(k):
+        return proxy_copy(proxy_ref, me, 2 * k, peer_of(2 * k))
+
+    def proxy_twin(k):
+        owner = lax.rem(me + n - 2 * k, n)
+        return proxy_copy(all_proxy.at[pl.ds(owner * pairs, pairs)], owner, 2 * k + 1, twin)
+
+    def proxy_start(k, carry):
+        proxy_far(k).start()
+        return carry
+
+    def proxy_pass(k, carry):
+        proxy_far(k).wait()
+        proxy_twin(k).start()
+        return carry
+
+    def proxy_wait(k, carry):
+        proxy_twin(k).wait()
+        return carry
+
+    lax.fori_loop(1, n // 2, proxy_start, 0)
+    own_twin = proxy_copy(proxy_ref, me, 1, twin)
+    own_twin.start()
     all_proxy[pl.ds(me * pairs, pairs)] = proxy_ref[...]
 
     lane8 = lax.broadcasted_iota(jnp.int32, (8, 128), 1)
@@ -196,7 +248,7 @@
                 low, basis_in_ref[c], (((1,), (1,)), ((), ())), preferred_element_type=jnp.float32
             )
             got = jnp.where(lane8[:1] < 64, got[0:1], got[1:2])
-            mom_all[step, pl.ds(me * clusters + c, 1), :] = got.astype(jnp.bfloat16).astype(jnp.float32)
+            low_exp[pl.ds(c, 1), :] = got
             return carry
 
         u_start, u_wait = halo(
@@ -207,19 +259,21 @@
         u_start()
         for c in range(clusters):
             moment(c, 0)
-        own = mom_all.at[step, pl.ds(me * clusters, clusters)]
+        mom_bf[step, me] = low_exp[...].astype(jnp.bfloat16)
+        own = mom_bf.at[step, me]
         mom_start, mom_wait = to_all(MOMENT + step, lambda p: own, own)
         mom_start()
         return u_wait, mom_wait
 
     def apply(step, u_wait, mom_wait):
         mom_wait()
+        mom_all[...] = mom_bf[step].astype(jnp.float32).reshape(mom_all.shape)
 
         def far_terms(group, carry):
             for q in range(TERM_UNROLL):
                 p = group * TERM_UNROLL + q
-                picked_a = mom_all[step, pl.ds(task_ref[1, p], 1), :]
-                picked_b = mom_all[step, pl.ds(task_ref[1, half + p], 1), :]
+                picked_a = mom_all[pl.ds(task_ref[1, p], 1), :]
+                picked_b = mom_all[pl.ds(task_ref[1, half + p], 1), :]
                 low = jnp.where(row8 == 0, picked_a, picked_b).astype(jnp.bfloat16)
                 got = jnp.dot(low, coupled[p], preferred_element_type=jnp.float32)
                 for k in range(2):
@@ -296,11 +350,15 @@
         start()
         dots_recv[index, me] = message
         wait()
-        return [dots_recv[index, :, q, :] for q in range(len(values))]
+        dots_flat[...] = dots_recv[index, :, 0, :]
+        got = dots_flat[...]
+        return [jnp.broadcast_to(got[:, q : q + 1], got.shape) for q in range(len(values))]
 
     add = lambda x: jnp.sum(x, axis=0, keepdims=True)
 
     geo_wait()
+    for load in loads:
+        load.wait()
 
     def near_build(r, carry):
         sources = [wide_geo[near_ref[t, r]] for t in range(near_count)]
@@ -319,15 +377,19 @@
                 near_mats[at, 1, lo:hi, 128:256] = adjoint - adjoint * (growth / ratio)
         return carry
 
-    lax.fori_loop(0, clusters, near_build, 0)
-
+    cut = clusters // 2
+    lax.fori_loop(0, cut, near_build, 0)
+    lax.fori_loop(1, n // 2, proxy_pass, 0)
     norm_wait()
     rhs_sq = add(dots_recv[0, :, 0, :])
     first = rhs / jnp.sqrt(rhs_sq / entries + eps)
     wide_u[0, :, pl.ds(clusters, clusters), :] = first
     u_wait, mom_wait = send_density(0)
 
-    proxy_wait()
+    lax.fori_loop(cut, clusters, near_build, 0)
+
+    own_twin.wait()
+    lax.fori_loop(1, n // 2, proxy_wait, 0)
     terms[...] = jnp.zeros_like(terms)
     row = lax.broadcasted_iota(jnp.int32, spreader.shape, 0)
     lane = lax.broadcasted_iota(jnp.int32, spreader.shape, 1)
@@ -425,6 +487,7 @@
     f32, bf16 = jnp.float32, jnp.bfloat16
     vmem = pl.BlockSpec(memory_space=pltpu.VMEM)
     smem = pl.BlockSpec(memory_space=pltpu.SMEM)
+    hbm = pl.BlockSpec(memory_space=pl.ANY)
     second, third, hess = pl.pallas_call(
         functools.partial(kernel, n),
         out_shape=(
@@ -432,7 +495,7 @@
             jax.ShapeDtypeStruct((2, clusters, members), f32),
             jax.ShapeDtypeStruct((8, 128), f32),
         ),
-        in_specs=[smem, smem] + [vmem] * 7,
+        in_specs=[smem, smem, vmem, vmem, hbm, vmem, hbm, hbm, vmem],
         out_specs=(vmem, vmem, vmem),
         scratch_shapes=[
             pltpu.VMEM((3 * clusters, 8, members), f32),
@@ -440,17 +503,23 @@
             pltpu.VMEM((clusters * near_count, 2, members, 2 * members), f32),
             pltpu.VMEM((tasks // 2, 2 * rank, 4 * rank), bf16),
             pltpu.VMEM((2, 2, 3 * clusters, members), f32),
-            pltpu.VMEM((2, total_clusters, 2 * rank), f32),
+            pltpu.VMEM((2, n, clusters, 2 * rank), bf16),
+            pltpu.VMEM((total_clusters, 2 * rank), f32),
             pltpu.VMEM((width, 2 * rank), f32),
             pltpu.VMEM((2, total_clusters, 2 * rank), f32),
             pltpu.VMEM((2, n, clusters, 2 * rank), f32),
-            pltpu.VMEM((3, 16, 128), f32),
-            pltpu.VMEM((3, n, 16, 128), f32),
+            pltpu.VMEM((3, 1, 128), f32),
+            pltpu.VMEM((3, n, 1, 128), f32),
             pltpu.VMEM((2, clusters, members), f32),
             pltpu.VMEM((2, clusters, members), f32),
             pltpu.VMEM((2, tasks // 2, 2 * rank), f32),
             pltpu.VMEM((clusters, 2 * rank), f32),
+            pltpu.VMEM((n, 128), f32),
             pltpu.VMEM((48, 896), bf16),
+            pltpu.VMEM((clusters, members, 8), f32),
+            pltpu.VMEM((clusters, 2 * rank, members), bf16),
+            pltpu.VMEM((clusters, 2 * rank, members), bf16),
+            pltpu.SemaphoreType.DMA((3,)),
             pltpu.SemaphoreType.DMA((8, n)),
             pltpu.SemaphoreType.DMA((8, n)),
             pltpu.SemaphoreType.DMA((3, 2)),

time: 79.3 us -> 71 us (0.90)
  Pallas kernels: 70.7 us -> 62.4 us
    pallas_call x1, Pallas kernels: 70.7 us -> 62.4 us  [shards(): pl.pallas_call(functools.partial(kernel, n), out_shape=(jax.ShapeDtypeStr...]
where the time goes in v3:
time: 71 us; the launch traced here: 70.7 us
  Pallas kernels  62.4 us (88%)
  local copies, waits for them, and re-layouts  5.85 us (8%)
  other arithmetic  1.69 us (2%)
  between operations  0.77 us (1%)
    pallas_call x1, Pallas kernels, shards(): pl.pallas_call(functools.partial(kernel, n), out_shape=(jax.ShapeDtypeStr...  62.4 us
    unnamed x19, local copies, waits for them, and re-layouts  3.61 us
    slice x1, other arithmetic, features(): points[5]  1.43 us

profile of v3, /device:TPU:0, one launch (start us, length us, event | category | flops | bytes accessed | tf_op | source)
XLA Modules:
  0.0 70.7 jit_solution(2965416050494904920)
XLA Ops:
  0.6 1.4 %fusion.1 = (f32[1,2048]{1,0:T(1,128)S(1)}, f32[1,2048]{1,0:T(1,128)S(1)}, f32[1,2048]{1,0:T(1,128)S(1)}, f32[1,2048]{1,0:T(1,128)S(1)}) fusion(f32[6,2048]{1,0:T(8,128)} %param.8), kind=kLoop, calls=%fused_computation.26 | loop fusion | flops 4096 | bytes 57344 | tf_op jit(solution)/shard_map/slice | solution.py:35
  2.1 0.8 %slice_bitcast_fusion = f32[1,3,16,128]{3,1,2,0:T(4,128)S(1)} fusion(f32[6,2048]{1,0:T(8,128)} %param.8), kind=kLoop, calls=%fused_computation.1 | loop fusion | bytes 49152
  3.0 0.0 copy-start
  3.0 0.0 copy-start.1
  3.0 0.3 copy.19
  3.3 0.0 copy-start.3
  3.4 0.7 %copy-done.3 = f32[6,1024]{1,0:T(8,128)S(1)} copy-done((f32[6,1024]{1,0:T(8,128)S(1)}, f32[6,1024]{1,0:T(8,128)}, u32[]{:S(2)}) %copy-start.3) | copy-done | bytes 24600
  4.1 0.2 slice_bitcast_fusion.2
  4.4 0.0 copy-start.4
  4.4 0.1 stack.45
  4.4 0.7 copy-done.4
  5.1 0.0 slice-start
  5.1 0.7 slice-done
  5.8 0.0 copy-start.5
  5.8 0.7 copy-done.5
  6.5 0.0 copy-start.2
  6.5 0.0 copy-done
  6.5 0.0 copy-done.1
  6.5 0.7 copy-done.2
  7.2 62.4 %shard_map.94 = (f32[2,16,128]{2,1,0:T(8,128)S(1)}, f32[2,16,128]{2,1,0:T(8,128)S(1)}, f32[8,128]{1,0:T(8,128)S(1)}) custom-call(s32[4,16]{1,0:T(4,128)S(1)} %add_select_fusion.near_ref, s32[2,192]{1,0:T(2,128)S(1)} %copy-done.2, f32[2,16,128]{2,1,0:T(8,128)S(1)} %bitcast.42, f32[16,8,128]{2,1,0:T(8,128)S(1)} %bitcast.40, f32[16,128,8]{2,1,0:T(8,128)S(1)} %bitcast.37, ...), custom_call_target="tpu_custom_call" | custom-call | tf_op jit(solution)/shard_map/pallas_call | solution.py:491
  69.5 0.6 copy_bitcast_fusion.1
  70.2 0.5 slice_bitcast_fusion.3
  (12 shorter events, 0.1 us)
Async XLA Ops:
  3.0 3.5 %copy-start = (bf16[16,2,64,128]{3,2,1,0:T(8,128)(2,1)S(1)}, bf16[16,2,64,128]{3,2,1,0:T(8,128)(2,1)}, u32[]{:S(2)}) copy-start(bf16[16,2,64,128]{3,2,1,0:T(8,128)(2,1)} %param.10) | copy-start | bytes 1572868
  3.0 3.5 %copy-start.1 = (bf16[16,2,64,128]{3,2,1,0:T(8,128)(2,1)S(1)}, bf16[16,2,64,128]{3,2,1,0:T(8,128)(2,1)}, u32[]{:S(2)}) copy-start(bf16[16,2,64,128]{3,2,1,0:T(8,128)(2,1)} %param.11) | copy-start | bytes 1572868
  3.3 0.8 %copy-start.3 = (f32[6,1024]{1,0:T(8,128)S(1)}, f32[6,1024]{1,0:T(8,128)}, u32[]{:S(2)}) copy-start(f32[6,1024]{1,0:T(8,128)} %param.9) | copy-start | bytes 73732
  4.4 0.7 %copy-start.4 = (f32[2,2048]{1,0:T(2,128)S(1)}, f32[2,2048]{1,0:T(2,128)}, u32[]{:S(2)}) copy-start(f32[2,2048]{1,0:T(2,128)} %param.7) | copy-start | bytes 49156
  5.1 0.7 slice-start
  5.8 0.7 copy-start.5
  6.5 0.7 copy-start.2

commit v4 on v3

--- a/solution.py
+++ b/solution.py
@@ -13,10 +13,10 @@
 eps = 1e-06
 MESH = pl.DeviceIdType.MESH
 
-FAR_UNROLL = 8
+FAR_UNROLL = 16
 FAR_CHUNK = 32
-NEAR_CHUNK = 32
-TERM_UNROLL = 16
+NEAR_CHUNK = 16
+TERM_UNROLL = 32
 UNROLL = 1
 
 PROXY, NORM, MOMENT, EXPAND, DOTS = 0, 1, 2, 4, 6
@@ -429,8 +429,9 @@
 
     lax.fori_loop(0, half // FAR_UNROLL, far_build, 0)
 
+    ff = total(first * first)
     image = apply(0, u_wait, mom_wait)
-    ff, fw = total(first * first), total(first * image)
+    fw = total(first * image)
     c1 = safe(fw, ff)
     left_over = image - c1 * first
     ff, fw, c1, rr, fr = exchange(1, [ff, fw, c1, total(left_over * left_over), total(first * left_over)])
@@ -442,8 +443,8 @@
     wide_u[1, :, pl.ds(clusters, clusters), :] = second
     u_wait, mom_wait = send_density(1)
 
+    ff, fv, vv = total(first * first), total(first * second), total(second * second)
     image = apply(1, u_wait, mom_wait)
-    ff, fv, vv = total(first * first), total(first * second), total(second * second)
     fw, vw = total(first * image), total(second * image)
     c1 = safe(fw, ff)
     left_over = image - c1 * first

time: 71 us -> 69.4 us (0.977)
  Pallas kernels: 62.4 us -> 60.7 us
    pallas_call x1, Pallas kernels: 62.4 us -> 60.7 us  [shards(): pl.pallas_call(functools.partial(kernel, n), out_shape=(jax.ShapeDtypeStr...]
where the time goes in v4:
time: 69.4 us; the launch traced here: 69 us
  Pallas kernels  60.7 us (87%)
  local copies, waits for them, and re-layouts  5.85 us (8%)
  other arithmetic  1.69 us (2%)
  between operations  0.77 us (1%)
    pallas_call x1, Pallas kernels, shards(): pl.pallas_call(functools.partial(kernel, n), out_shape=(jax.ShapeDtypeStr...  60.7 us
    unnamed x19, local copies, waits for them, and re-layouts  3.61 us
    slice x1, other arithmetic, features(): points[5]  1.43 us

profile of v4, /device:TPU:0, one launch (start us, length us, event | category | flops | bytes accessed | tf_op | source)
XLA Modules:
  0.0 69.0 jit_solution(16003016285157315022)
XLA Ops:
  0.6 1.4 %fusion.1 = (f32[1,2048]{1,0:T(1,128)S(1)}, f32[1,2048]{1,0:T(1,128)S(1)}, f32[1,2048]{1,0:T(1,128)S(1)}, f32[1,2048]{1,0:T(1,128)S(1)}) fusion(f32[6,2048]{1,0:T(8,128)} %param.8), kind=kLoop, calls=%fused_computation.26 | loop fusion | flops 4096 | bytes 57344 | tf_op jit(solution)/shard_map/slice | solution.py:35
  2.1 0.8 %slice_bitcast_fusion = f32[1,3,16,128]{3,1,2,0:T(4,128)S(1)} fusion(f32[6,2048]{1,0:T(8,128)} %param.8), kind=kLoop, calls=%fused_computation.1 | loop fusion | bytes 49152
  3.0 0.0 copy-start
  3.0 0.0 copy-start.1
  3.0 0.3 copy.19
  3.3 0.0 copy-start.3
  3.4 0.7 %copy-done.3 = f32[6,1024]{1,0:T(8,128)S(1)} copy-done((f32[6,1024]{1,0:T(8,128)S(1)}, f32[6,1024]{1,0:T(8,128)}, u32[]{:S(2)}) %copy-start.3) | copy-done | bytes 24600
  4.1 0.2 slice_bitcast_fusion.2
  4.4 0.0 copy-start.4
  4.4 0.1 stack.45
  4.4 0.7 copy-done.4
  5.1 0.0 slice-start
  5.1 0.7 slice-done
  5.8 0.0 copy-start.5
  5.8 0.7 copy-done.5
  6.5 0.0 copy-start.2
  6.5 0.0 copy-done
  6.5 0.0 copy-done.1
  6.5 0.7 copy-done.2
  7.2 60.7 %shard_map.94 = (f32[2,16,128]{2,1,0:T(8,128)S(1)}, f32[2,16,128]{2,1,0:T(8,128)S(1)}, f32[8,128]{1,0:T(8,128)S(1)}) custom-call(s32[4,16]{1,0:T(4,128)S(1)} %add_select_fusion.near_ref, s32[2,192]{1,0:T(2,128)S(1)} %copy-done.2, f32[2,16,128]{2,1,0:T(8,128)S(1)} %bitcast.42, f32[16,8,128]{2,1,0:T(8,128)S(1)} %bitcast.40, f32[16,128,8]{2,1,0:T(8,128)S(1)} %bitcast.37, ...), custom_call_target="tpu_custom_call" | custom-call | tf_op jit(solution)/shard_map/pallas_call | solution.py:492
  67.9 0.6 copy_bitcast_fusion.1
  68.5 0.5 slice_bitcast_fusion.3
  (12 shorter events, 0.1 us)
Async XLA Ops:
  3.0 3.5 %copy-start = (bf16[16,2,64,128]{3,2,1,0:T(8,128)(2,1)S(1)}, bf16[16,2,64,128]{3,2,1,0:T(8,128)(2,1)}, u32[]{:S(2)}) copy-start(bf16[16,2,64,128]{3,2,1,0:T(8,128)(2,1)} %param.10) | copy-start | bytes 1572868
  3.0 3.5 %copy-start.1 = (bf16[16,2,64,128]{3,2,1,0:T(8,128)(2,1)S(1)}, bf16[16,2,64,128]{3,2,1,0:T(8,128)(2,1)}, u32[]{:S(2)}) copy-start(bf16[16,2,64,128]{3,2,1,0:T(8,128)(2,1)} %param.11) | copy-start | bytes 1572868
  3.3 0.8 %copy-start.3 = (f32[6,1024]{1,0:T(8,128)S(1)}, f32[6,1024]{1,0:T(8,128)}, u32[]{:S(2)}) copy-start(f32[6,1024]{1,0:T(8,128)} %param.9) | copy-start | bytes 73732
  4.4 0.7 %copy-start.4 = (f32[2,2048]{1,0:T(2,128)S(1)}, f32[2,2048]{1,0:T(2,128)}, u32[]{:S(2)}) copy-start(f32[2,2048]{1,0:T(2,128)} %param.7) | copy-start | bytes 49156
  5.1 0.7 slice-start
  5.8 0.7 copy-start.5
  6.5 0.7 copy-start.2
